TPU v7x, 32 devices: a whole 2x2x4 slice. The times are simulated.
32 devices in a mesh: freq: 4 (over x, core), order: 8 (over z, y).
Axes of the slice: x: 2, y: 2, z: 4, core: 2. Of those that a mesh axis runs over, the one named last changes fastest.
Arguments:
- harmonics: bfloat16 [32, 16, 2, 4096], P(None, 'order'), may hold values from -6 to 6
- legendre: bfloat16 [16, 4096, 64], P('order'), may hold values from -0.09375 to 0.09375
- beam_window: float32 [4, 4096], replicated, may hold values from 0.2 to 1
- order_ids: int32 [16], replicated, may hold values from 0 to 4095, as said below
- noise_weight: float32 [4, 64, 8192], P('freq', 'order'), may hold values from 0.3 to 3
Outputs:
- applied: float32 [32, 16, 2, 4096], P('freq', 'order')
Inputs may be any that keep to these rules, and one draw needn't show every extreme that they name: `order_ids`: all distinct; slots 2k and 2k + 1 hold the orders m and 4095 - m for some m < 2048; one pair holds the orders 0 and 4095.
All inputs are finite; a program needn't handle non-finite values.
Results may differ from a plain program's by a relative error of at most 0.0027.
Values may be sent and summed in bfloat16 or wider, within the bound.
A program may use at most 64 MiB of HBM per device.

v0:
```python
import math

import jax
import jax.numpy as jnp
from jax import lax
from jax.sharding import PartitionSpec as P

ORD_DEV = 2


def make_table(order_ids, nlon):
    steps = jnp.arange(nlon, dtype=jnp.int32)
    turns = order_ids[:, None] * steps[None, :] % nlon
    angle = turns.astype(jnp.float32) * (2.0 * math.pi / nlon)
    factor = jnp.where(order_ids == 0, 1.0, 2.0).astype(jnp.float32)[:, None]
    return jnp.stack([factor * jnp.cos(angle), -factor * jnp.sin(angle)], 1).astype(jnp.bfloat16)


def on_device(harmonics, legendre, beam_window, order_ids, noise_weight):
    degrees = harmonics.shape[3]
    nlon = noise_weight.shape[2]
    orders_all = order_ids.shape[0]
    first_slot = lax.axis_index("order") * ORD_DEV
    local_ids = lax.dynamic_slice_in_dim(order_ids, first_slot, ORD_DEV, 0)
    live_mask = (jnp.arange(degrees, dtype=jnp.int32)[None, :] >= local_ids[:, None]).astype(
        jnp.float32
    )
    own_beam = lax.dynamic_index_in_dim(beam_window, lax.axis_index("freq"), 0, keepdims=False)
    own_shaping = (own_beam[None, :] * live_mask)[None, :, None, :]
    smoothed = (harmonics.astype(jnp.float32) * own_shaping).astype(jnp.bfloat16)
    columns = jnp.einsum(
        "bocl,olr->bocr", smoothed, legendre, preferred_element_type=jnp.float32
    ).astype(jnp.bfloat16)
    dft_table = make_table(order_ids, nlon)
    fwd_scale = 1.0 / math.sqrt(2.0 * orders_all)
    back_scale = 1.0 / math.sqrt(1.0 * nlon)
    pixel_weights = noise_weight[0]
    field = (
        jnp.einsum(
            "bocr,ocj->brj",
            lax.all_to_all(columns, "order", split_axis=3, concat_axis=1, tiled=True),
            dft_table,
            preferred_element_type=jnp.float32,
        )
        * fwd_scale
    )
    weighted = (field * pixel_weights[None]).astype(jnp.bfloat16)
    summed = jnp.einsum("brj,ocj->bocr", weighted, dft_table, preferred_element_type=jnp.float32)
    band_terms = (summed * back_scale).astype(jnp.bfloat16)
    returned = lax.all_to_all(band_terms, "order", split_axis=1, concat_axis=3, tiled=True)
    shared = lax.all_to_all(returned[None], "freq", split_axis=1, concat_axis=0, tiled=True)
    total = jnp.zeros((shared.shape[1], ORD_DEV, 2, degrees), jnp.float32)
    for group in range(shared.shape[0]):
        projected = jnp.einsum(
            "bocr,olr->bocl", shared[group], legendre, preferred_element_type=jnp.float32
        )
        total = total + projected * (beam_window[group][None, :] * live_mask)[None, :, None, :]
    return total


def solution(mesh):
    return jax.shard_map(
        on_device,
        mesh=mesh,
        in_specs=(
            P(None, "order", None, None),
            P("order", None, None),
            P(),
            P(),
            P("freq", "order", None),
        ),
        out_specs=P("freq", "order", None, None),
        check_vma=False,
    )
```

profile of v0, /device:TPU:0, one launch (start us, length us, event | category | flops | bytes accessed | tf_op | source)
XLA Modules:
  0.0 42.9 jit_solution(15537241873491286911)
XLA Ops:
  0.0 1.1 %fusion.37 = (f32[1,4096]{1,0:T(1,128)S(1)}, f32[1,4096]{1,0:T(1,128)S(1)}, f32[1,4096]{1,0:T(1,128)S(1)}, f32[1,4096]{1,0:T(1,128)S(1)}, f32[1,4096]{1,0:T(1,128)S(1)}) fusion(f32[4,4096]{1,0:T(4,128)} %param.7, s32[]{:T(128)S(6)} %select_n.32), kind=kLoop, calls=%fused_computation.57 | loop fusion | bytes 163844 | tf_op jit(solution)/shard_map/slice | solution.py:57
  1.1 0.7 %dynamic_slice.7 = s32[2]{0:T(128)S(1)} dynamic-slice(s32[16]{0:T(128)} %param.8, s32[]{:T(128)S(6)} %select_n.31), dynamic_slice_sizes={2} | dynamic-slice | bytes 20 | tf_op jit(solution)/shard_map/dynamic_slice | solution.py:24
  1.9 0.1 fusion.29
  2.0 2.3 %multiply_convert_fusion = bf16[32,2,2,4096]{3,2,1,0:T(2,128)(2,1)S(1)} fusion(bf16[32,2,2,4096]{3,2,1,0:T(2,128)(2,1)} %param.5, f32[2,4096]{1,0:T(2,128)S(1)} %get-tuple-element.17), kind=kLoop, calls=%fused_computation.12 | loop fusion | flops 1572864 | bytes 2129920 | tf_op jit(solution)/shard_map/convert_element_type | solution.py:30
  4.4 0.9 %fusion.11 = bf16[32,2,2,64]{3,0,2,1:T(8,128)(2,1)S(1)} fusion(bf16[2,4096,64]{1,2,0:T(8,128)(2,1)S(1)} %copy-done, bf16[32,2,2,4096]{3,2,1,0:T(2,128)(2,1)S(1)} %multiply_convert_fusion), kind=kOutput, calls=%fused_computation.18 | convolution fusion | flops 67117056 | bytes 2113536 | tf_op jit(solution)/shard_map/bocl,olr->bocr/dot_general | solution.py:31
  5.3 0.1 copy.17
  5.4 0.7 %reshape.306 = bf16[8,2,512]{2,1,0:T(2,128)(2,1)} reshape(bf16[64,2,2,32]{3,2,1,0:T(2,128)(2,1)S(1)} %bitcast.94) | data formatting | bytes 32768
  6.1 7.3 %all-to-all-start = ((bf16[8,2,512]{2,1,0:T(2,128)(2,1)}), bf16[8,2,512]{2,1,0:T(2,128)(2,1)S(1)}, u32[]{:S(2)}, u32[]{:S(2)}) async-start(bf16[8,2,512]{2,1,0:T(2,128)(2,1)} %reshape.306), calls=%async_computation | async-start | bytes 32768 | tf_op jit(solution)/shard_map/all_to_all | solution.py:41
  13.4 2.3 %multiply_convert_fusion.2 = (bf16[16,1,8192]{2,0,1:T(8,128)(2,1)S(1)}, bf16[16,1,8192]{2,0,1:T(8,128)(2,1)S(1)}) fusion(s32[16]{0:T(128)S(1)} %copy-done.2, f32[16]{0:T(128)S(1)} %get-tuple-element.20, f32[16]{0:T(128)S(1)} %get-tuple-element.21), kind=kLoop, calls=%fused_computation.35 | loop fusion | flops 2359296 | bytes 524480 | tf_op jit(solution)/shard_map/convert
  15.8 4.2 %all-to-all-done = bf16[8,2,512]{2,1,0:T(2,128)(2,1)S(1)} async-done(((bf16[8,2,512]{2,1,0:T(2,128)(2,1)}), bf16[8,2,512]{2,1,0:T(2,128)(2,1)S(1)}, u32[]{:S(2)}, u32[]{:S(2)}) %all-to-all-start) | async-done | bytes 16416 | tf_op jit(solution)/shard_map/all_to_all | solution.py:41
  20.0 0.1 reshape.307
  20.1 4.5 %fusion.10 = bf16[32,16,2,8]{0,1,3,2:T(8,128)(2,1)S(1)} fusion(f32[8,8192]{1,0:T(8,128)S(1)} %multiply_bitcast_fusion, bf16[16,1,8192]{2,0,1:T(8,128)(2,1)S(1)} %get-tuple-element.19, bf16[16,1,8192]{2,0,1:T(8,128)(2,1)S(1)} %get-tuple-element.18, bf16[32,16,2,8]{0,3,2,1:T(8,128)(2,1)S(1)} %bitcast.103), kind=kOutput, calls=%fused_computation.16 | convolution fusion | flops 273956864 | bytes 819200 | tf_op jit(solution)/shard_map/brj,ocj->bocr/dot_general | solution.py:48
  24.7 0.1 reshape.308
  24.8 8.9 %all_to_all.45 = bf16[8,2,512]{2,1,0:T(2,128)(2,1)S(1)} all-to-all(bf16[8,2,512]{2,1,0:T(2,128)(2,1)S(1)} %reshape.308), channel_id=1, replica_groups=mesh['freq'=4,'order'=8] {'order'}, dimensions={0} | all-to-all | bytes 32768 | tf_op jit(solution)/shard_map/all_to_all | solution.py:50
  33.7 0.1 reshape.309
  33.8 0.1 copy.23
  33.9 0.1 reshape.310
  34.0 6.4 %all_to_all.46 = bf16[4,2,1024]{2,1,0:T(2,128)(2,1)S(1)} all-to-all(bf16[4,2,1024]{2,1,0:T(2,128)(2,1)S(1)} %reshape.310), channel_id=1, replica_groups=mesh['freq'=4,'order'=8] {'freq'}, dimensions={0} | all-to-all | bytes 32768 | tf_op jit(solution)/shard_map/all_to_all | solution.py:51
  40.5 0.1 reshape.311
  40.6 0.3 convolution_multiply_fusion.3
  40.9 0.3 fusion.5
  41.1 0.3 fusion.4
  41.4 0.3 fusion.6
  41.7 1.2 %copy.29 = f32[8,2,2,4096]{3,2,1,0:T(2,128)} copy(f32[8,2,2,4096]{3,0,2,1:T(8,128)S(1)} %fusion.6) | data formatting | bytes 1048576 | tf_op jit(solution)/shard_map/add | solution.py:57
  (14 shorter events, 0.1 us)
Async XLA Ops:
  0.0 4.3 %copy-start = (bf16[2,4096,64]{1,2,0:T(8,128)(2,1)S(1)}, bf16[2,4096,64]{1,2,0:T(8,128)(2,1)}, u32[]{:S(2)}) copy-start(bf16[2,4096,64]{1,2,0:T(8,128)(2,1)} %param.6) | copy-start | bytes 3145732
  4.3 9.1 %copy-start.2 = (s32[16]{0:T(128)S(1)}, s32[16]{0:T(128)}, u32[]{:S(2)}) copy-start(s32[16]{0:T(128)} %param.8) | copy-start | bytes 196
  4.4 11.4 %copy-start.1 = (f32[1,8,8192]{2,1,0:T(8,128)S(1)}, f32[1,8,8192]{2,1,0:T(8,128)}, u32[]{:S(2)}) copy-start(f32[1,8,8192]{2,1,0:T(8,128)} %param.9) | copy-start | bytes 786436
  6.1 13.9 %all-to-all-start = ((bf16[8,2,512]{2,1,0:T(2,128)(2,1)}), bf16[8,2,512]{2,1,0:T(2,128)(2,1)S(1)}, u32[]{:S(2)}, u32[]{:S(2)}) async-start(bf16[8,2,512]{2,1,0:T(2,128)(2,1)} %reshape.306), calls=%async_computation | async-start | bytes 32768 | tf_op jit(solution)/shard_map/all_to_all | solution.py:41
where the time goes:
time: 43.2 us; the launch traced here: 42.9 us
  blocking collectives  15.4 us (36%)
  starting transfers between devices  7.28 us (17%)
  matrix products  6.44 us (15%)
  other arithmetic  4.78 us (11%)
  local copies, waits for them, and re-layouts  4.6 us (11%)
  waiting for transfers between devices  4.2 us (10%)
    all_to_all x1, blocking collectives, on_device(): lax.all_to_all(band_terms, 'order', split_axis=1, concat_axis=3, tiled=True)  8.94 us
    all_to_all x1, starting transfers between devices, on_device(): lax.all_to_all(columns, 'order', split_axis=3, concat_axis=1, tiled=True)  7.28 us
    all_to_all x1, blocking collectives, on_device(): lax.all_to_all(returned[None], 'freq', split_axis=1, concat_axis=0, tiled...  6.43 us
    dot_general x1, matrix products, on_device(): jnp.einsum('brj,ocj->bocr', weighted, dft_table, preferred_element_type=j...  4.46 us
    all_to_all x1, waiting for transfers between devices, on_device(): lax.all_to_all(columns, 'order', split_axis=3, concat_axis=1, tiled=True)  4.2 us
    convert_element_type x1, other arithmetic, on_device(): (harmonics.astype(jnp.float32) * own_shaping).astype(jnp.bfloat16)  2.31 us
    another operation x1, other arithmetic  2.3 us
    unnamed x12, local copies, waits for them, and re-layouts  1.25 us
  transfers between devices with their start and end apart: 1, of which 1 were waited for; matrix products, arithmetic and copies ran while one was open for 5% of the time, Pallas kernels for 0%

commit v1 on v0

v1 whole, which is shorter than its diff:
```python
import functools
import math

import jax
import jax.numpy as jnp
from jax import lax
from jax.experimental import pallas as pl
from jax.experimental.pallas import tpu as pltpu
from jax.sharding import PartitionSpec as P

MESH = pl.DeviceIdType.MESH
NT = (((1,), (1,)), ((), ()))
LANES = 128
F32 = jnp.float32
BF16 = jnp.bfloat16


def sin_cos_turns(step, period):
    turns = step.astype(F32) * (4.0 / period)
    quarter = jnp.floor(turns + 0.5)
    x = (turns - quarter) * (0.5 * math.pi)
    y = x * x
    sin = x * (1.0 + y * (-1.0 / 6 + y * (1.0 / 120 + y * (-1.0 / 5040 + y * (1.0 / 362880)))))
    cos = 1.0 + y * (-0.5 + y * (1.0 / 24 + y * (-1.0 / 720 + y * (1.0 / 40320 - y * (1.0 / 3628800)))))
    quad = quarter.astype(jnp.int32) % 4
    odd = quad % 2 == 1
    c = jnp.where(odd, sin, cos)
    s = jnp.where(odd, cos, sin)
    c = jnp.where((quad == 1) | (quad == 2), -c, c)
    s = jnp.where(quad >= 2, -s, s)
    return c, s


def build_table(ids, wide, table, rows, nlon):
    shape = (rows, LANES)
    row = lax.broadcasted_iota(jnp.int32, shape, 0)
    lane = lax.broadcasted_iota(jnp.int32, shape, 1)
    order = jnp.zeros(shape, jnp.int32)
    for slot in range(rows // 2):
        order = jnp.where(row // 2 == slot, ids[slot], order)
    c, s = sin_cos_turns((order * lane + (row % 2) * (nlon // 4)) % nlon, nlon)
    factor = jnp.where(order == 0, 1.0, 2.0).astype(F32)
    c, s = c * factor, s * factor
    doublings = int(math.log2(nlon // LANES))
    reach = jnp.left_shift(LANES, jnp.minimum(lane, doublings))
    rc, rs = sin_cos_turns((order * reach) % nlon, nlon)
    cos_parts, sin_parts = [c], [s]
    for level in range(doublings):
        bc = jnp.broadcast_to(rc[:, level : level + 1], shape)
        bs = jnp.broadcast_to(rs[:, level : level + 1], shape)
        new_cos = [c * bc - s * bs for c, s in zip(cos_parts, sin_parts)]
        if level < doublings - 1:
            sin_parts = sin_parts + [s * bc + c * bs for c, s in zip(cos_parts, sin_parts)]
        cos_parts = cos_parts + new_cos
    for part, c in enumerate(cos_parts):
        rounded = c.astype(BF16)
        table[:, part * LANES : (part + 1) * LANES] = rounded
        wide[:, part * LANES : (part + 1) * LANES] = rounded.astype(F32)


def gather_kernel(
    nf, no, ids, beam, harm_hbm, leg_hbm, noise_hbm, z_ref,
    harm, leg, noise, wide, table, gram, spread, xs, xr, vs, vr, flipped,
    load_sem, send1, recv1, send2, recv2,
):
    maps, od, _, degrees = harm.shape
    lats, nlon = noise.shape[1], noise.shape[2]
    all_lats = leg.shape[1]
    rows = no * od * 2
    half = maps * 2
    total = nf * no
    myf, me = lax.axis_index("freq"), lax.axis_index("order")
    lin = myf * no + me

    loads = [
        pltpu.make_async_copy(harm_hbm, harm, load_sem.at[0]),
        pltpu.make_async_copy(leg_hbm, leg, load_sem.at[1]),
        pltpu.make_async_copy(noise_hbm, noise, load_sem.at[2]),
    ]
    for load in loads:
        load.start()

    barrier = pltpu.get_barrier_semaphore()

    def greet(k, carry):
        to = (lin + k) % total
        pl.semaphore_signal(barrier, inc=1, device_id=(to // no, to % no), device_id_type=MESH)
        return carry

    lax.fori_loop(1, total, greet, 0)

    build_table(ids, wide, table, rows, nlon)

    own_beam = beam[pl.ds(myf, 1), :]
    loads[0].wait()
    loads[1].wait()
    step = 512
    parts = []
    for o in range(od):
        degree = lax.broadcasted_iota(jnp.int32, (1, degrees), 1)
        shaping = jnp.where(degree >= ids[me * od + o], own_beam, 0.0)
        acc = jnp.zeros((all_lats, half), F32)
        for at in range(0, degrees, step):
            cut = slice(at, at + step)
            piece = harm[:, o, :, cut].astype(F32) * shaping[:, cut].reshape(1, 1, step)
            piece = piece.reshape(half, step).astype(BF16)
            acc = acc + lax.dot_general(leg[o, :, cut], piece, NT, preferred_element_type=F32)
        parts.append(acc)
    columns = jnp.concatenate(parts, axis=1).astype(BF16).astype(F32)
    xs[...] = columns.reshape(no, lats, od * half)
    xr[me] = xs[me]

    pl.semaphore_wait(barrier, total - 1)

    def copy1(k):
        to = (me + k) % no
        return pltpu.make_async_remote_copy(
            xs.at[to], xr.at[me], send1.at[to], recv1.at[me],
            device_id=(myf, to), device_id_type=MESH,
        )

    def arrive1(k):
        frm = (me + k) % no
        return pltpu.make_async_remote_copy(
            xs.at[frm], xr.at[frm], send1.at[frm], recv1.at[frm],
            device_id=(myf, frm), device_id_type=MESH,
        )

    lax.fori_loop(1, no, lambda k, c: (copy1(k).start(), c)[1], 0)

    loads[2].wait()
    wide_step = 1024

    def gram_step(i, acc):
        cut = pl.ds(pl.multiple_of(i * wide_step, wide_step), wide_step)
        left = wide[:, cut][:, None, :] * noise[0, :, cut][None, :, :]
        left = left.reshape(rows * lats, wide_step).astype(BF16)
        return acc + lax.dot_general(left, table[:, cut], NT, preferred_element_type=F32)

    acc = lax.fori_loop(
        0, nlon // wide_step, gram_step, jnp.zeros((rows * lats, rows), F32)
    )
    gram[...] = acc * (1.0 / math.sqrt(2.0 * no * od) / math.sqrt(1.0 * nlon))

    span = no * LANES
    p = lax.broadcasted_iota(jnp.int32, (rows, span), 0)
    q = lax.broadcasted_iota(jnp.int32, (rows, span), 1)
    lane_q = q % LANES
    fan = (p == (q // LANES) * (2 * od) + (lane_q // half) * 2 + lane_q % 2).astype(F32).astype(BF16)

    def expand(value):
        high = value.astype(BF16)
        low = (value - high.astype(F32)).astype(BF16)
        return jnp.dot(high, fan, preferred_element_type=F32) + jnp.dot(
            low, fan, preferred_element_type=F32
        )

    ahead = spread.shape[0] == rows * lats
    if ahead:
        spread[...] = expand(gram[...])

    def settle1(k, c):
        arrive1(k).wait_recv()
        return c

    lax.fori_loop(1, no, settle1, 0)

    lane = lax.broadcasted_iota(jnp.int32, (lats, LANES), 1)
    even = lane % 2 == 0
    first = lane < half

    def mix(d, get):
        sums = []
        for s in range(2 * od):
            t = get(s, 0) * xr[0]
            for o in range(1, no):
                t = t + get(s, o) * xr[o]
            t = t + pltpu.roll(t, half, 1)
            t = t + jnp.where(even, pltpu.roll(t, LANES - 1, 1), pltpu.roll(t, 1, 1))
            sums.append(t)
        out = jnp.where(first, jnp.where(even, sums[0], sums[1]), jnp.where(even, sums[2], sums[3]))
        vs[d] = out.astype(BF16).astype(F32)

    group = 2 * od * lats
    if ahead:
        for d in range(no):
            mix(d, lambda s, o: spread[d * group + s * lats : d * group + (s + 1) * lats, o * LANES : (o + 1) * LANES])
    else:
        def late(d, c):
            spread[...] = expand(gram[pl.ds(pl.multiple_of(d * group, group), group), :])
            mix(d, lambda s, o: spread[s * lats : (s + 1) * lats, o * LANES : (o + 1) * LANES])
            return c
        lax.fori_loop(0, no, late, 0)

    vr[myf, me] = vs[me]

    def copy2(k):
        to = (lin + k) % total
        return pltpu.make_async_remote_copy(
            vs.at[to % no], vr.at[myf, me], send2.at[to], recv2.at[lin],
            device_id=(to // no, to % no), device_id_type=MESH,
        )

    def arrive2(k):
        frm = (lin + k) % total
        return pltpu.make_async_remote_copy(
            vs.at[frm % no], vr.at[frm // no, frm % no], send2.at[frm], recv2.at[frm],
            device_id=(frm // no, frm % no), device_id_type=MESH,
        )

    lax.fori_loop(1, total, lambda k, c: (copy2(k).start(), c)[1], 0)

    def settle2(k, c):
        arrive2(k).wait_recv()
        return c

    lax.fori_loop(1, total, settle2, 0)

    keep = half // nf
    for f in range(nf):
        flipped[f] = vr[f].reshape(all_lats, od * half).T
        for o in range(od):
            at = pl.multiple_of(o * half + myf * keep, keep)
            z_ref[o, f] = flipped[f, pl.ds(at, keep), :].astype(BF16)

    def drain(k, c):
        copy2(k).wait_send()
        return c

    lax.fori_loop(1, no, lambda k, c: (copy1(k).wait_send(), c)[1], 0)
    lax.fori_loop(1, total, drain, 0)


def project_kernel(ids, z_ref, beam, leg, out):
    od, nf, keep, all_lats = z_ref.shape
    width = leg.shape[2]
    me = lax.axis_index("order")
    degree = lax.broadcasted_iota(jnp.int32, (1, width), 1) + pl.program_id(0) * width
    for o in range(od):
        wide = jnp.dot(
            z_ref[o].reshape(nf * keep, all_lats), leg[o], preferred_element_type=F32
        )
        total = wide[0:keep] * beam[0:1, :]
        for f in range(1, nf):
            total = total + wide[f * keep : (f + 1) * keep] * beam[f : f + 1, :]
        total = jnp.where(degree >= ids[me * od + o], total, 0.0)
        out[:, o] = total.reshape(keep // 2, 2, width)


def on_device(nf, no, harmonics, legendre, beam_window, order_ids, noise_weight):
    maps, od, _, degrees = harmonics.shape
    _, lats, nlon = noise_weight.shape
    all_lats = legendre.shape[2]
    rows, half, total = no * od * 2, maps * 2, nf * no
    keep = half // nf
    leg = jnp.swapaxes(legendre, 1, 2)
    smem = pl.BlockSpec(memory_space=pltpu.SMEM)
    vmem = pl.BlockSpec(memory_space=pltpu.VMEM)
    hbm = pl.BlockSpec(memory_space=pl.ANY)
    span = no * LANES
    ahead = rows * lats * span * 4 <= 8 * 2**20
    dma = pltpu.SemaphoreType.DMA
    z = pl.pallas_call(
        functools.partial(gather_kernel, nf, no),
        out_shape=jax.ShapeDtypeStruct((od, nf, keep, all_lats), BF16),
        in_specs=[smem, vmem, hbm, hbm, hbm],
        out_specs=vmem,
        scratch_shapes=[
            pltpu.VMEM(harmonics.shape, BF16),
            pltpu.VMEM(leg.shape, BF16),
            pltpu.VMEM(noise_weight.shape, F32),
            pltpu.VMEM((rows, nlon), F32),
            pltpu.VMEM((rows, nlon), BF16),
            pltpu.VMEM((rows * lats, rows), F32),
            pltpu.VMEM((rows * lats if ahead else 2 * od * lats, span), F32),
            pltpu.VMEM((no, lats, od * half), F32),
            pltpu.VMEM((no, lats, od * half), F32),
            pltpu.VMEM((no, lats, od * half), F32),
            pltpu.VMEM((nf, no, lats, od * half), F32),
            pltpu.VMEM((nf, od * half, all_lats), F32),
            dma((3,)),
            dma((no,)),
            dma((no,)),
            dma((total,)),
            dma((total,)),
        ],
        compiler_params=pltpu.CompilerParams(
            collective_id=0, has_side_effects=True, vmem_limit_bytes=52 * 2**20
        ),
        name="exchange",
    )(order_ids, beam_window, harmonics, leg, noise_weight)
    width = 1024
    return pl.pallas_call(
        project_kernel,
        grid=(degrees // width,),
        out_shape=jax.ShapeDtypeStruct((maps // nf, od, 2, degrees), F32),
        in_specs=[
            smem,
            pl.BlockSpec(z.shape, lambda i: (0, 0, 0, 0)),
            pl.BlockSpec((nf, width), lambda i: (0, i)),
            pl.BlockSpec((od, all_lats, width), lambda i: (0, 0, i)),
        ],
        out_specs=pl.BlockSpec((maps // nf, od, 2, width), lambda i: (0, 0, 0, i)),
        compiler_params=pltpu.CompilerParams(vmem_limit_bytes=32 * 2**20),
        name="project",
    )(order_ids, z, beam_window, leg)


def solution(mesh):
    sizes = dict(mesh.shape)
    return jax.shard_map(
        functools.partial(on_device, sizes["freq"], sizes["order"]),
        mesh=mesh,
        in_specs=(
            P(None, "order", None, None),
            P("order", None, None),
            P(),
            P(),
            P("freq", "order", None),
        ),
        out_specs=P("freq", "order", None, None),
        check_vma=False,
    )
```

time: 43.2 us -> 24.9 us (0.58)
  Pallas kernels: 0 us -> 21 us
  blocking collectives: 15.4 us -> 0 us
  starting transfers between devices: 7.28 us -> 0 us
  matrix products: 6.44 us -> 0 us
  other arithmetic: 4.78 us -> 0 us
  waiting for transfers between devices: 4.2 us -> 0 us
  local copies, waits for them, and re-layouts: 4.6 us -> 3.67 us
    pallas_call x0 -> x2, Pallas kernels: none -> 21 us  [the longest x1 18.4 us: on_device(): pl.pallas_call(functools.partial(gather_kernel, nf, no), out_shape=jax.Sh...]
    all_to_all x2 -> x0, blocking collectives: 15.4 us -> none  [the longest x1 8.94 us: on_device(): lax.all_to_all(band_terms, 'order', split_axis=1, concat_axis=3, tiled=True)]
    all_to_all x1 -> x0, starting transfers between devices: 7.28 us -> none  [on_device(): lax.all_to_all(columns, 'order', split_axis=3, concat_axis=1, tiled=True)]
    dot_general x6 -> x0, matrix products: 6.44 us -> none  [the longest x1 4.46 us: on_device(): jnp.einsum('brj,ocj->bocr', weighted, dft_table, preferred_element_type=j...]
    all_to_all x1 -> x0, waiting for transfers between devices: 4.2 us -> none  [on_device(): lax.all_to_all(columns, 'order', split_axis=3, concat_axis=1, tiled=True)]
    unnamed x12 -> x10, local copies, waits for them, and re-layouts: 1.25 us -> 3.67 us
    convert_element_type x1 -> x0, other arithmetic: 2.31 us -> none  [on_device(): (harmonics.astype(jnp.float32) * own_shaping).astype(jnp.bfloat16)]
    another operation x1 -> x0, other arithmetic: 2.3 us -> none
  transfers between devices with their start and end apart: 1 -> 0, of which waited for: 1 -> 0; matrix products, arithmetic and copies ran while one was open for 5% -> 0% of each run, Pallas kernels for 0% -> 0%
where the time goes in v1:
time: 24.9 us; the launch traced here: 24.7 us
  Pallas kernels  21 us (84%)
  local copies, waits for them, and re-layouts  3.67 us (15%)
    pallas_call x1, Pallas kernels, on_device(): pl.pallas_call(functools.partial(gather_kernel, nf, no), out_shape=jax.Sh...  18.4 us
    unnamed x10, local copies, waits for them, and re-layouts  3.67 us
    pallas_call x1, Pallas kernels, on_device(): pl.pallas_call(project_kernel, grid=(degrees // width,), out_shape=jax.Sh...  2.6 us

profile of v1, /device:TPU:0, one launch (start us, length us, event | category | flops | bytes accessed | tf_op | source)
XLA Modules:
  0.0 24.7 jit_solution(7538311871023617305)
XLA Ops:
  0.0 0.0 copy-start.4
  0.0 0.7 %copy-done.4 = s32[16]{0:T(128)S(1)} copy-done((s32[16]{0:T(128)S(1)}, s32[16]{0:T(128)}, u32[]{:S(2)}) %copy-start.4) | copy-done | bytes 88
  0.7 0.0 copy-start.1
  0.7 1.2 %copy-done.1 = bf16[32,2,2,4096]{3,2,1,0:T(2,128)(2,1)S(1)} copy-done((bf16[32,2,2,4096]{3,2,1,0:T(2,128)(2,1)S(1)}, bf16[32,2,2,4096]{3,2,1,0:T(2,128)(2,1)}, u32[]{:S(2)}) %copy-start.1) | copy-done | bytes 1048600
  1.9 0.0 copy-start.2
  1.9 0.8 %copy-done.2 = f32[4,4096]{1,0:T(4,128)S(1)} copy-done((f32[4,4096]{1,0:T(4,128)S(1)}, f32[4,4096]{1,0:T(4,128)}, u32[]{:S(2)}) %copy-start.2) | copy-done | bytes 65560
  2.7 0.0 copy-start.3
  2.7 0.9 %copy-done.3 = f32[1,8,8192]{2,1,0:T(8,128)S(1)} copy-done((f32[1,8,8192]{2,1,0:T(8,128)S(1)}, f32[1,8,8192]{2,1,0:T(8,128)}, u32[]{:S(2)}) %copy-start.3) | copy-done | bytes 262168
  3.7 0.0 copy-start
  3.7 18.4 %exchange.1.z_ref = bf16[2,4,16,64]{3,2,1,0:T(8,128)(2,1)S(1)} custom-call(s32[16]{0:T(128)S(1)} %copy-done.4, f32[4,4096]{1,0:T(4,128)S(1)} %copy-done.2, bf16[32,2,2,4096]{3,2,1,0:T(2,128)(2,1)S(1)} %copy-done.1, bf16[2,64,4096]{2,1,0:T(8,128)(2,1)} %bitcast.1, f32[1,8,8192]{2,1,0:T(8,128)S(1)} %copy-done.3), custom_call_target="tpu_custom_call" | custom-call | tf_op jit(solution)/shard_map/exchange/pallas_call | solution.py:263
  22.1 0.0 copy-done
  22.1 2.6 %project.1 = f32[8,2,2,4096]{3,2,1,0:T(2,128)} custom-call(s32[16]{0:T(128)S(1)} %copy-done.4, bf16[2,4,16,64]{3,2,1,0:T(8,128)(2,1)S(1)} %exchange.1.z_ref, f32[4,4096]{1,0:T(4,128)S(1)} %copy-done.2, bf16[2,64,4096]{2,1,0:T(8,128)(2,1)S(1)} %bitcast.2), custom_call_target="tpu_custom_call" | custom-call | tf_op jit(solution)/shard_map/project/pallas_call | solution.py:293
Async XLA Ops:
  0.0 0.7 %copy-start.4 = (s32[16]{0:T(128)S(1)}, s32[16]{0:T(128)}, u32[]{:S(2)}) copy-start(s32[16]{0:T(128)} %ids.3) | copy-start | bytes 196
  0.7 1.2 %copy-start.1 = (bf16[32,2,2,4096]{3,2,1,0:T(2,128)(2,1)S(1)}, bf16[32,2,2,4096]{3,2,1,0:T(2,128)(2,1)}, u32[]{:S(2)}) copy-start(bf16[32,2,2,4096]{3,2,1,0:T(2,128)(2,1)} %harm_hbm.1) | copy-start | bytes 3145732
  1.9 0.8 %copy-start.2 = (f32[4,4096]{1,0:T(4,128)S(1)}, f32[4,4096]{1,0:T(4,128)}, u32[]{:S(2)}) copy-start(f32[4,4096]{1,0:T(4,128)} %beam.3) | copy-start | bytes 196612
  2.7 0.9 %copy-start.3 = (f32[1,8,8192]{2,1,0:T(8,128)S(1)}, f32[1,8,8192]{2,1,0:T(8,128)}, u32[]{:S(2)}) copy-start(f32[1,8,8192]{2,1,0:T(8,128)} %noise_hbm.1) | copy-start | bytes 786436
  3.7 18.4 %copy-start = (bf16[2,4096,64]{1,2,0:T(8,128)(2,1)S(1)}, bf16[2,4096,64]{1,2,0:T(8,128)(2,1)}, u32[]{:S(2)}) copy-start(bf16[2,4096,64]{1,2,0:T(8,128)(2,1)} %param.6) | copy-start | bytes 3145732

commit v2 on v1

v2 whole, which is shorter than its diff:
```python
import functools
import math

import jax
import jax.numpy as jnp
from jax import lax
from jax.experimental import pallas as pl
from jax.experimental.pallas import tpu as pltpu
from jax.sharding import PartitionSpec as P

MESH = pl.DeviceIdType.MESH
NT = (((1,), (1,)), ((), ()))
LANES = 128
F32 = jnp.float32
BF16 = jnp.bfloat16


def sin_cos_turns(step, period):
    turns = step.astype(F32) * (4.0 / period)
    quarter = jnp.floor(turns + 0.5)
    x = (turns - quarter) * (0.5 * math.pi)
    y = x * x
    sin = x * (1.0 + y * (-1.0 / 6 + y * (1.0 / 120 + y * (-1.0 / 5040 + y * (1.0 / 362880)))))
    cos = 1.0 + y * (-0.5 + y * (1.0 / 24 + y * (-1.0 / 720 + y * (1.0 / 40320 - y * (1.0 / 3628800)))))
    quad = quarter.astype(jnp.int32) % 4
    odd = quad % 2 == 1
    c = jnp.where(odd, sin, cos)
    s = jnp.where(odd, cos, sin)
    c = jnp.where((quad == 1) | (quad == 2), -c, c)
    s = jnp.where(quad >= 2, -s, s)
    return c, s


def build_table(ids, wide, table, rows, nlon):
    shape = (rows, LANES)
    row = lax.broadcasted_iota(jnp.int32, shape, 0)
    lane = lax.broadcasted_iota(jnp.int32, shape, 1)
    order = jnp.zeros(shape, jnp.int32)
    for slot in range(rows // 2):
        order = jnp.where(row // 2 == slot, ids[slot], order)
    c, s = sin_cos_turns((order * lane + (row % 2) * (nlon // 4)) % nlon, nlon)
    factor = jnp.where(order == 0, 1.0, 2.0).astype(F32)
    c, s = c * factor, s * factor
    doublings = int(math.log2(nlon // LANES))
    reach = jnp.left_shift(LANES, jnp.minimum(lane, doublings))
    rc, rs = sin_cos_turns((order * reach) % nlon, nlon)
    cos_parts, sin_parts = [c], [s]
    for level in range(doublings):
        bc = jnp.broadcast_to(rc[:, level : level + 1], shape)
        bs = jnp.broadcast_to(rs[:, level : level + 1], shape)
        new_cos = [c * bc - s * bs for c, s in zip(cos_parts, sin_parts)]
        if level < doublings - 1:
            sin_parts = sin_parts + [s * bc + c * bs for c, s in zip(cos_parts, sin_parts)]
        cos_parts = cos_parts + new_cos
    for part, c in enumerate(cos_parts):
        rounded = c.astype(BF16)
        table[:, part * LANES : (part + 1) * LANES] = rounded
        wide[:, part * LANES : (part + 1) * LANES] = rounded.astype(F32)


def wrap(value, n):
    return jnp.where(value >= n, value - n, value)


def gather_kernel(
    nf, no, ids_hbm, beam_hbm, harm_hbm, leg_hbm, noise_hbm, out,
    ids, beam, harm, leg, noise, flat, wide, table, gram, spread, xs, xr, vs, vr, flipped,
    shaping_ref, stage, load_sem, send1, recv1, send2, recv2, out_sem,
):
    maps, od, tiles2, _ = harm.shape
    tiles = tiles2 // 2
    lats, nlon = noise.shape[1], noise.shape[2]
    all_lats = leg.shape[1]
    rows = no * od * 2
    half = maps * 2
    total = nf * no
    myf, me = lax.axis_index("freq"), lax.axis_index("order")
    lin = myf * no + me

    def peers_order(act):
        if no <= 16:
            for k in range(1, no):
                act(wrap(me + k, no))
        else:
            lax.fori_loop(1, no, lambda k, c: (act(wrap(me + k, no)), c)[1], 0)

    def peers_all(act):
        for g in range(nf):
            f = wrap(myf + g, nf)
            low = 1 if g == 0 else 0
            if total <= 64:
                for k in range(low, no):
                    act(f, wrap(me + k, no))
            else:
                lax.fori_loop(low, no, lambda k, c: (act(f, wrap(me + k, no)), c)[1], 0)

    loads = [
        pltpu.make_async_copy(ids_hbm, ids, load_sem.at[0]),
        pltpu.make_async_copy(harm_hbm, harm, load_sem.at[1]),
        pltpu.make_async_copy(beam_hbm, beam, load_sem.at[2]),
        pltpu.make_async_copy(leg_hbm, leg, load_sem.at[3]),
        pltpu.make_async_copy(noise_hbm, noise, load_sem.at[4]),
    ]
    for load in loads:
        load.start()

    barrier = pltpu.get_barrier_semaphore()

    def greet(f, o):
        pl.semaphore_signal(barrier, inc=1, device_id=(f, o), device_id_type=MESH)

    peers_all(greet)

    loads[0].wait()
    build_table(ids, wide, table, rows, nlon)

    loads[2].wait()
    degrees = beam.shape[1]
    degree = lax.broadcasted_iota(jnp.int32, (1, degrees), 1)
    for o in range(od):
        shaping_ref[o] = jnp.where(degree >= ids[me * od + o], beam[...], 0.0)
    loads[1].wait()
    loads[3].wait()
    step = 4
    parts = []
    for o in range(od):
        flat[o] = harm[:, o].astype(F32).reshape(maps * tiles2, LANES)
        shaping = shaping_ref[o, pl.ds(myf, 1), :]
        acc = jnp.zeros((all_lats, half), F32)
        for at in range(0, tiles, step):
            piece = jnp.concatenate(
                [
                    jnp.concatenate(
                        [
                            flat[o, pl.ds(t * 2 + c, maps, stride=tiles2), :]
                            * shaping[:, t * LANES : (t + 1) * LANES]
                            for t in range(at, at + step)
                        ],
                        axis=1,
                    )
                    for c in range(2)
                ],
                axis=0,
            ).astype(BF16)
            cut = slice(at * LANES, (at + step) * LANES)
            acc = acc + lax.dot_general(leg[o, :, cut], piece, NT, preferred_element_type=F32)
        parts.append(acc)
    columns = jnp.concatenate(parts, axis=1).astype(BF16).astype(F32)
    xs[...] = columns.reshape(no, lats, od * half)
    xr[me] = xs[me]

    pl.semaphore_wait(barrier, total - 1)

    def copy1(to):
        return pltpu.make_async_remote_copy(
            xs.at[to], xr.at[me], send1.at[to], recv1.at[me],
            device_id=(myf, to), device_id_type=MESH,
        )

    def arrive1(frm):
        pltpu.make_async_remote_copy(
            xs.at[frm], xr.at[frm], send1.at[frm], recv1.at[frm],
            device_id=(myf, frm), device_id_type=MESH,
        ).wait_recv()

    peers_order(lambda to: copy1(to).start())

    loads[4].wait()
    wide_step = 1024

    def gram_step(i, acc):
        cut = pl.ds(pl.multiple_of(i * wide_step, wide_step), wide_step)
        left = wide[:, cut][:, None, :] * noise[0, :, cut][None, :, :]
        left = left.reshape(rows * lats, wide_step).astype(BF16)
        return acc + lax.dot_general(left, table[:, cut], NT, preferred_element_type=F32)

    acc = lax.fori_loop(
        0, nlon // wide_step, gram_step, jnp.zeros((rows * lats, rows), F32)
    )
    gram[...] = acc * (1.0 / math.sqrt(2.0 * no * od) / math.sqrt(1.0 * nlon))

    span = no * LANES
    p = lax.broadcasted_iota(jnp.int32, (rows, span), 0)
    q = lax.broadcasted_iota(jnp.int32, (rows, span), 1)
    fan = (p == q // maps).astype(F32).astype(BF16)

    def expand(value):
        high = value.astype(BF16)
        low = (value - high.astype(F32)).astype(BF16)
        return jnp.dot(high, fan, preferred_element_type=F32) + jnp.dot(
            low, fan, preferred_element_type=F32
        )

    ahead = spread.shape[0] == rows * lats
    if ahead:
        spread[...] = expand(gram[...])

    peers_order(arrive1)

    part = lax.broadcasted_iota(jnp.int32, (lats, LANES), 1) // maps

    def mix(d, get):
        out = None
        for s in range(2 * od):
            t = get(s, 0) * xr[0]
            for o in range(1, no):
                t = t + get(s, o) * xr[o]
            t = t + pltpu.roll(t, half, 1)
            t = t + pltpu.roll(t, maps, 1)
            out = t if out is None else jnp.where(part == s, t, out)
        vs[d] = out.astype(BF16).astype(F32)

    group = 2 * od * lats
    if ahead:
        for d in range(no):
            mix(d, lambda s, o: spread[d * group + s * lats : d * group + (s + 1) * lats, o * LANES : (o + 1) * LANES])
    else:
        def late(d, c):
            spread[...] = expand(gram[pl.ds(pl.multiple_of(d * group, group), group), :])
            mix(d, lambda s, o: spread[s * lats : (s + 1) * lats, o * LANES : (o + 1) * LANES])
            return c
        lax.fori_loop(0, no, late, 0)

    vr[myf, me] = vs[me]

    def copy2(f, o):
        return pltpu.make_async_remote_copy(
            vs.at[o], vr.at[myf, me], send2.at[f * no + o], recv2.at[lin],
            device_id=(f, o), device_id_type=MESH,
        )

    def arrive2(f, o):
        frm = f * no + o
        pltpu.make_async_remote_copy(
            vs.at[o], vr.at[f, o], send2.at[frm], recv2.at[frm],
            device_id=(f, o), device_id_type=MESH,
        ).wait_recv()

    peers_all(lambda f, o: copy2(f, o).start())
    peers_all(arrive2)

    keep = maps // nf
    for f in range(nf):
        flipped[f] = vr[f].reshape(all_lats, od * half).T

    width = 1024
    copies = []
    for o in range(od):
        pieces = []
        for f in range(nf):
            for c in range(2):
                at = pl.multiple_of(o * half + c * maps + myf * keep, keep)
                pieces.append(flipped[f, pl.ds(at, keep), :])
        z = jnp.concatenate(pieces, axis=0).astype(BF16)
        for at in range(0, degrees, width):
            cut = slice(at, at + width)
            terms = jnp.dot(z, leg[o, :, cut], preferred_element_type=F32)
            sums = terms[0 : 2 * keep] * shaping_ref[o, 0:1, cut]
            for f in range(1, nf):
                sums = sums + terms[f * 2 * keep : (f + 1) * 2 * keep] * shaping_ref[o, f : f + 1, cut]
            for t in range(width // LANES):
                for c in range(2):
                    row = (at // LANES + t) * 2 + c
                    stage[o, pl.ds(row, keep, stride=tiles2), :] = sums[
                        c * keep : (c + 1) * keep, t * LANES : (t + 1) * LANES
                    ]
        for b in range(keep):
            copy = pltpu.make_async_copy(
                stage.at[o, pl.ds(b * tiles2, tiles2)], out.at[b, o], out_sem.at[o, b]
            )
            copy.start()
            copies.append(copy)

    peers_order(lambda to: copy1(to).wait_send())
    peers_all(lambda f, o: copy2(f, o).wait_send())
    for copy in copies:
        copy.wait()


def on_device(nf, no, harmonics, legendre, beam_window, order_ids, noise_weight):
    maps, od, _, degrees = harmonics.shape
    _, lats, nlon = noise_weight.shape
    all_lats = legendre.shape[2]
    rows, half, total = no * od * 2, maps * 2, nf * no
    keep = maps // nf
    tiles = degrees // LANES
    leg = jnp.swapaxes(legendre, 1, 2)
    harm = harmonics.reshape(maps, od, 2, tiles, LANES)
    harm = jnp.swapaxes(harm, 2, 3).reshape(maps, od, tiles * 2, LANES)
    hbm = pl.BlockSpec(memory_space=pltpu.HBM)
    span = no * LANES
    ahead = rows * lats * span * 4 <= 8 * 2**20
    dma = pltpu.SemaphoreType.DMA
    out = pl.pallas_call(
        functools.partial(gather_kernel, nf, no),
        out_shape=jax.ShapeDtypeStruct((keep, od, tiles * 2, LANES), F32),
        in_specs=[hbm, hbm, hbm, hbm, hbm],
        out_specs=hbm,
        scratch_shapes=[
            pltpu.SMEM(order_ids.shape, jnp.int32),
            pltpu.VMEM(beam_window.shape, F32),
            pltpu.VMEM(harm.shape, BF16),
            pltpu.VMEM(leg.shape, BF16),
            pltpu.VMEM(noise_weight.shape, F32),
            pltpu.VMEM((od, maps * tiles * 2, LANES), F32),
            pltpu.VMEM((rows, nlon), F32),
            pltpu.VMEM((rows, nlon), BF16),
            pltpu.VMEM((rows * lats, rows), F32),
            pltpu.VMEM((rows * lats if ahead else 2 * od * lats, span), F32),
            pltpu.VMEM((no, lats, od * half), F32),
            pltpu.VMEM((no, lats, od * half), F32),
            pltpu.VMEM((no, lats, od * half), F32),
            pltpu.VMEM((nf, no, lats, od * half), F32),
            pltpu.VMEM((nf, od * half, all_lats), F32),
            pltpu.VMEM((od, nf, degrees), F32),
            pltpu.VMEM((od, keep * tiles * 2, LANES), F32),
            dma((5,)),
            dma((no,)),
            dma((no,)),
            dma((total,)),
            dma((total,)),
            dma((od, keep)),
        ],
        compiler_params=pltpu.CompilerParams(
            collective_id=0, has_side_effects=True, vmem_limit_bytes=60 * 2**20
        ),
        name="operator",
    )(order_ids, beam_window, harm, leg, noise_weight)
    out = jnp.swapaxes(out.reshape(keep, od, tiles, 2, LANES), 2, 3)
    return out.reshape(keep, od, 2, degrees)


def solution(mesh):
    sizes = dict(mesh.shape)
    return jax.shard_map(
        functools.partial(on_device, sizes["freq"], sizes["order"]),
        mesh=mesh,
        in_specs=(
            P(None, "order", None, None),
            P("order", None, None),
            P(),
            P(),
            P("freq", "order", None),
        ),
        out_specs=P("freq", "order", None, None),
        check_vma=False,
    )
```

time: 24.9 us -> 20.3 us (0.82)
  Pallas kernels: 21 us -> 18.2 us
  local copies, waits for them, and re-layouts: 3.67 us -> 1.89 us
    pallas_call x1 -> x0, Pallas kernels: 2.6 us -> none  [on_device(): pl.pallas_call(project_kernel, grid=(degrees // width,), out_shape=jax.Sh...]
    unnamed x10 -> x1, local copies, waits for them, and re-layouts: 3.67 us -> 1.89 us
where the time goes in v2:
time: 20.3 us; the launch traced here: 20.1 us
  Pallas kernels  18.2 us (90%)
  local copies, waits for them, and re-layouts  1.89 us (9%)
    pallas_call x1, Pallas kernels, on_device(): pl.pallas_call(functools.partial(gather_kernel, nf, no), out_shape=jax.Sh...  18.2 us
    unnamed x1, local copies, waits for them, and re-layouts  1.89 us

profile of v2, /device:TPU:0, one launch (start us, length us, event | category | flops | bytes accessed | tf_op | source)
XLA Modules:
  0.0 20.1 jit_solution(17721798084946573656)
XLA Ops:
  0.0 18.2 %operator.1 = f32[8,2,64,128]{3,2,1,0:T(8,128)} custom-call(s32[16]{0:T(128)} %ids_hbm.1, f32[4,4096]{1,0:T(4,128)} %beam_hbm.1, bf16[32,2,64,128]{3,2,1,0:T(8,128)(2,1)} %bitcast.12, bf16[2,64,4096]{2,1,0:T(8,128)(2,1)} %bitcast.13, f32[1,8,8192]{2,1,0:T(8,128)} %noise_hbm.1), custom_call_target="tpu_custom_call" | custom-call | tf_op jit(solution)/shard_map/operator/pallas_call | solution.py:294
  18.2 1.9 %copy.9 = f32[8,2,2,4096]{3,2,1,0:T(2,128)} copy(f32[8,2,2,4096]{3,2,1,0:T(2,128)} %bitcast.11) | data formatting | bytes 1048576

commit v3 on v2

--- a/solution.py
+++ b/solution.py
@@ -22,8 +22,8 @@
     y = x * x
     sin = x * (1.0 + y * (-1.0 / 6 + y * (1.0 / 120 + y * (-1.0 / 5040 + y * (1.0 / 362880)))))
     cos = 1.0 + y * (-0.5 + y * (1.0 / 24 + y * (-1.0 / 720 + y * (1.0 / 40320 - y * (1.0 / 3628800)))))
-    quad = quarter.astype(jnp.int32) % 4
-    odd = quad % 2 == 1
+    quad = quarter.astype(jnp.int32) & 3
+    odd = (quad & 1) == 1
     c = jnp.where(odd, sin, cos)
     s = jnp.where(odd, cos, sin)
     c = jnp.where((quad == 1) | (quad == 2), -c, c)
@@ -37,13 +37,13 @@
     lane = lax.broadcasted_iota(jnp.int32, shape, 1)
     order = jnp.zeros(shape, jnp.int32)
     for slot in range(rows // 2):
-        order = jnp.where(row // 2 == slot, ids[slot], order)
-    c, s = sin_cos_turns((order * lane + (row % 2) * (nlon // 4)) % nlon, nlon)
+        order = jnp.where(row >= 2 * slot, ids[slot], order)
+    c, s = sin_cos_turns(lax.rem(order * lane + (row & 1) * (nlon // 4), nlon), nlon)
     factor = jnp.where(order == 0, 1.0, 2.0).astype(F32)
     c, s = c * factor, s * factor
     doublings = int(math.log2(nlon // LANES))
     reach = jnp.left_shift(LANES, jnp.minimum(lane, doublings))
-    rc, rs = sin_cos_turns((order * reach) % nlon, nlon)
+    rc, rs = sin_cos_turns(lax.rem(order * reach, nlon), nlon)
     cos_parts, sin_parts = [c], [s]
     for level in range(doublings):
         bc = jnp.broadcast_to(rc[:, level : level + 1], shape)
@@ -64,7 +64,7 @@
 
 def gather_kernel(
     nf, no, ids_hbm, beam_hbm, harm_hbm, leg_hbm, noise_hbm, out,
-    ids, beam, harm, leg, noise, flat, wide, table, gram, spread, xs, xr, vs, vr, flipped,
+    ids, beam, harm, leg, noise, flat, wide, table, gram, fan, spread, xs, xr, vs, vr, flipped,
     shaping_ref, stage, load_sem, send1, recv1, send2, recv2, out_sem,
 ):
     maps, od, tiles2, _ = harm.shape
@@ -113,6 +113,12 @@
 
     loads[0].wait()
     build_table(ids, wide, table, rows, nlon)
+
+    span = no * LANES
+    p = lax.broadcasted_iota(jnp.int32, (rows, span), 0) * maps
+    q = lax.broadcasted_iota(jnp.int32, (rows, span), 1)
+    fan_half = ((q >= p) & (q < p + maps)).astype(F32).astype(BF16)
+    fan[...] = jnp.concatenate([fan_half, fan_half], axis=0)
 
     loads[2].wait()
     degrees = beam.shape[1]
@@ -170,8 +176,9 @@
 
     def gram_step(i, acc):
         cut = pl.ds(pl.multiple_of(i * wide_step, wide_step), wide_step)
-        left = wide[:, cut][:, None, :] * noise[0, :, cut][None, :, :]
-        left = left.reshape(rows * lats, wide_step).astype(BF16)
+        weight = noise[0, :, cut]
+        left = [(wide[row : row + 1, cut] * weight) for row in range(rows)]
+        left = jnp.concatenate(left, axis=0).astype(BF16)
         return acc + lax.dot_general(left, table[:, cut], NT, preferred_element_type=F32)
 
     acc = lax.fori_loop(
@@ -179,17 +186,11 @@
     )
     gram[...] = acc * (1.0 / math.sqrt(2.0 * no * od) / math.sqrt(1.0 * nlon))
 
-    span = no * LANES
-    p = lax.broadcasted_iota(jnp.int32, (rows, span), 0)
-    q = lax.broadcasted_iota(jnp.int32, (rows, span), 1)
-    fan = (p == q // maps).astype(F32).astype(BF16)
-
     def expand(value):
         high = value.astype(BF16)
         low = (value - high.astype(F32)).astype(BF16)
-        return jnp.dot(high, fan, preferred_element_type=F32) + jnp.dot(
-            low, fan, preferred_element_type=F32
-        )
+        both = jnp.concatenate([high, low], axis=1)
+        return jnp.dot(both, fan[...], preferred_element_type=F32)
 
     ahead = spread.shape[0] == rows * lats
     if ahead:
@@ -197,7 +198,46 @@
 
     peers_order(arrive1)
 
-    part = lax.broadcasted_iota(jnp.int32, (lats, LANES), 1) // maps
+    keep = maps // nf
+    folds = lats // nf
+    lane = lax.broadcasted_iota(jnp.int32, (lats, LANES), 1)
+    sub = lax.broadcasted_iota(jnp.int32, (lats, LANES), 0)
+    part = lane // maps
+    slot = lax.rem(lane, maps) // keep
+    own_slot = slot == lax.rem(sub, nf)
+
+    def pack(d, value):
+        turned = [value]
+        for k in range(1, nf):
+            turned.append(
+                jnp.where(
+                    slot >= k,
+                    pltpu.roll(value, k * keep, 1),
+                    pltpu.roll(value, LANES + k * keep - maps, 1),
+                )
+            )
+        for f in range(nf):
+            own = turned[-f % nf]
+            for at in range(1, nf):
+                own = jnp.where(slot == at, turned[(at - f) % nf], own)
+            own = jnp.where(own_slot, own, 0.0)
+            shift = 1
+            while shift < nf:
+                own = own + pltpu.roll(own, lats - shift, 0)
+                shift *= 2
+            for row in range(folds):
+                vs[f, d, row : row + 1, :] = own[row * nf : row * nf + 1]
+
+    def unpack(f, o):
+        value = jnp.broadcast_to(vr[f, o, 0:1, :], (lats, LANES))
+        for row in range(1, folds):
+            value = jnp.where(sub >= row * nf, jnp.broadcast_to(vr[f, o, row : row + 1, :], (lats, LANES)), value)
+        value = jnp.where(own_slot, value, 0.0)
+        shift = 1
+        while shift < nf:
+            value = value + pltpu.roll(value, LANES - shift * keep, 1)
+            shift *= 2
+        return value
 
     def mix(d, get):
         out = None
@@ -208,7 +248,7 @@
             t = t + pltpu.roll(t, half, 1)
             t = t + pltpu.roll(t, maps, 1)
             out = t if out is None else jnp.where(part == s, t, out)
-        vs[d] = out.astype(BF16).astype(F32)
+        pack(d, out.astype(BF16).astype(F32))
 
     group = 2 * od * lats
     if ahead:
@@ -221,27 +261,26 @@
             return c
         lax.fori_loop(0, no, late, 0)
 
-    vr[myf, me] = vs[me]
+    vr[myf, me] = vs[myf, me]
 
     def copy2(f, o):
         return pltpu.make_async_remote_copy(
-            vs.at[o], vr.at[myf, me], send2.at[f * no + o], recv2.at[lin],
+            vs.at[f, o], vr.at[myf, me], send2.at[f * no + o], recv2.at[lin],
             device_id=(f, o), device_id_type=MESH,
         )
 
     def arrive2(f, o):
         frm = f * no + o
         pltpu.make_async_remote_copy(
-            vs.at[o], vr.at[f, o], send2.at[frm], recv2.at[frm],
+            vs.at[f, o], vr.at[f, o], send2.at[frm], recv2.at[frm],
             device_id=(f, o), device_id_type=MESH,
         ).wait_recv()
 
     peers_all(lambda f, o: copy2(f, o).start())
     peers_all(arrive2)
 
-    keep = maps // nf
     for f in range(nf):
-        flipped[f] = vr[f].reshape(all_lats, od * half).T
+        flipped[f] = jnp.concatenate([unpack(f, o) for o in range(no)], axis=0).T
 
     width = 1024
     copies = []
@@ -249,8 +288,8 @@
         pieces = []
         for f in range(nf):
             for c in range(2):
-                at = pl.multiple_of(o * half + c * maps + myf * keep, keep)
-                pieces.append(flipped[f, pl.ds(at, keep), :])
+                at = o * half + c * maps
+                pieces.append(flipped[f, at : at + keep, :])
         z = jnp.concatenate(pieces, axis=0).astype(BF16)
         for at in range(0, degrees, width):
             cut = slice(at, at + width)
@@ -306,11 +345,12 @@
             pltpu.VMEM((rows, nlon), F32),
             pltpu.VMEM((rows, nlon), BF16),
             pltpu.VMEM((rows * lats, rows), F32),
+            pltpu.VMEM((rows * 2, span), BF16),
             pltpu.VMEM((rows * lats if ahead else 2 * od * lats, span), F32),
             pltpu.VMEM((no, lats, od * half), F32),
             pltpu.VMEM((no, lats, od * half), F32),
-            pltpu.VMEM((no, lats, od * half), F32),
-            pltpu.VMEM((nf, no, lats, od * half), F32),
+            pltpu.VMEM((nf, no, lats // nf, od * half), F32),
+            pltpu.VMEM((nf, no, lats // nf, od * half), F32),
             pltpu.VMEM((nf, od * half, all_lats), F32),
             pltpu.VMEM((od, nf, degrees), F32),
             pltpu.VMEM((od, keep * tiles * 2, LANES), F32),

time: 20.3 us -> 20.1 us (level)
  no operation moved by 1% of the time
where the time goes in v3:
time: 20.1 us; the launch traced here: 19.9 us
  Pallas kernels  18 us (90%)
  local copies, waits for them, and re-layouts  1.89 us (9%)
    pallas_call x1, Pallas kernels, on_device(): pl.pallas_call(functools.partial(gather_kernel, nf, no), out_shape=jax.Sh...  18 us
    unnamed x1, local copies, waits for them, and re-layouts  1.89 us

profile of v3, /device:TPU:0, one launch (start us, length us, event | category | flops | bytes accessed | tf_op | source)
XLA Modules:
  0.0 19.9 jit_solution(7036597722544667908)
XLA Ops:
  0.0 18.0 %operator.1 = f32[8,2,64,128]{3,2,1,0:T(8,128)} custom-call(s32[16]{0:T(128)} %ids_hbm.1, f32[4,4096]{1,0:T(4,128)} %beam_hbm.1, bf16[32,2,64,128]{3,2,1,0:T(8,128)(2,1)} %bitcast.12, bf16[2,64,4096]{2,1,0:T(8,128)(2,1)} %bitcast.13, f32[1,8,8192]{2,1,0:T(8,128)} %noise_hbm.1), custom_call_target="tpu_custom_call" | custom-call | tf_op jit(solution)/shard_map/operator/pallas_call | solution.py:333
  18.0 1.9 %copy.9 = f32[8,2,2,4096]{3,2,1,0:T(2,128)} copy(f32[8,2,2,4096]{3,2,1,0:T(2,128)} %bitcast.11) | data formatting | bytes 1048576

commit v4 on v3

--- a/solution.py
+++ b/solution.py
@@ -31,31 +31,32 @@
     return c, s
 
 
-def build_table(ids, wide, table, rows, nlon):
-    shape = (rows, LANES)
+def build_table(ids, wide, table, slots, nlon):
+    shape = (slots, LANES)
     row = lax.broadcasted_iota(jnp.int32, shape, 0)
     lane = lax.broadcasted_iota(jnp.int32, shape, 1)
     order = jnp.zeros(shape, jnp.int32)
-    for slot in range(rows // 2):
-        order = jnp.where(row >= 2 * slot, ids[slot], order)
-    c, s = sin_cos_turns(lax.rem(order * lane + (row & 1) * (nlon // 4), nlon), nlon)
+    for slot in range(slots):
+        order = jnp.where(row >= slot, ids[slot], order)
+    c, s = sin_cos_turns(lax.rem(order * lane, nlon), nlon)
     factor = jnp.where(order == 0, 1.0, 2.0).astype(F32)
-    c, s = c * factor, s * factor
+    wide[0:slots, 0:LANES] = c * factor
+    wide[slots : 2 * slots, 0:LANES] = -s * factor
     doublings = int(math.log2(nlon // LANES))
     reach = jnp.left_shift(LANES, jnp.minimum(lane, doublings))
     rc, rs = sin_cos_turns(lax.rem(order * reach, nlon), nlon)
-    cos_parts, sin_parts = [c], [s]
     for level in range(doublings):
         bc = jnp.broadcast_to(rc[:, level : level + 1], shape)
         bs = jnp.broadcast_to(rs[:, level : level + 1], shape)
-        new_cos = [c * bc - s * bs for c, s in zip(cos_parts, sin_parts)]
-        if level < doublings - 1:
-            sin_parts = sin_parts + [s * bc + c * bs for c, s in zip(cos_parts, sin_parts)]
-        cos_parts = cos_parts + new_cos
-    for part, c in enumerate(cos_parts):
-        rounded = c.astype(BF16)
-        table[:, part * LANES : (part + 1) * LANES] = rounded
-        wide[:, part * LANES : (part + 1) * LANES] = rounded.astype(F32)
+        for part in range(2**level):
+            old = slice(part * LANES, (part + 1) * LANES)
+            new = slice((part + 2**level) * LANES, (part + 1 + 2**level) * LANES)
+            c, s = wide[0:slots, old], wide[slots : 2 * slots, old]
+            wide[0:slots, new] = c * bc + s * bs
+            wide[slots : 2 * slots, new] = s * bc - c * bs
+    rounded = wide[...].astype(BF16)
+    table[...] = rounded
+    wide[...] = rounded.astype(F32)
 
 
 def wrap(value, n):
@@ -64,7 +65,7 @@
 
 def gather_kernel(
     nf, no, ids_hbm, beam_hbm, harm_hbm, leg_hbm, noise_hbm, out,
-    ids, beam, harm, leg, noise, flat, wide, table, gram, fan, spread, xs, xr, vs, vr, flipped,
+    ids, beam, harm, leg, noise, wide, table, gram, fan, spread, xs, xr, vs, vr, flipped,
     shaping_ref, stage, load_sem, send1, recv1, send2, recv2, out_sem,
 ):
     maps, od, tiles2, _ = harm.shape
@@ -112,12 +113,13 @@
     peers_all(greet)
 
     loads[0].wait()
-    build_table(ids, wide, table, rows, nlon)
+    build_table(ids, wide, table, no * od, nlon)
 
     span = no * LANES
-    p = lax.broadcasted_iota(jnp.int32, (rows, span), 0) * maps
+    p = lax.broadcasted_iota(jnp.int32, (rows, span), 0)
     q = lax.broadcasted_iota(jnp.int32, (rows, span), 1)
-    fan_half = ((q >= p) & (q < p + maps)).astype(F32).astype(BF16)
+    begin = jnp.where(p < no * od, p * half, (p - no * od) * half + maps)
+    fan_half = ((q >= begin) & (q < begin + maps)).astype(F32).astype(BF16)
     fan[...] = jnp.concatenate([fan_half, fan_half], axis=0)
 
     loads[2].wait()
@@ -127,20 +129,20 @@
         shaping_ref[o] = jnp.where(degree >= ids[me * od + o], beam[...], 0.0)
     loads[1].wait()
     loads[3].wait()
-    step = 4
+    step = 8
     parts = []
     for o in range(od):
-        flat[o] = harm[:, o].astype(F32).reshape(maps * tiles2, LANES)
         shaping = shaping_ref[o, pl.ds(myf, 1), :]
         acc = jnp.zeros((all_lats, half), F32)
         for at in range(0, tiles, step):
+            block = harm[:, o, 2 * at : 2 * (at + step), :].astype(F32)
+            block = jnp.swapaxes(block, 0, 1)
             piece = jnp.concatenate(
                 [
                     jnp.concatenate(
                         [
-                            flat[o, pl.ds(t * 2 + c, maps, stride=tiles2), :]
-                            * shaping[:, t * LANES : (t + 1) * LANES]
-                            for t in range(at, at + step)
+                            block[2 * t + c] * shaping[:, (at + t) * LANES : (at + t + 1) * LANES]
+                            for t in range(step)
                         ],
                         axis=1,
                     )
@@ -181,8 +183,9 @@
         left = jnp.concatenate(left, axis=0).astype(BF16)
         return acc + lax.dot_general(left, table[:, cut], NT, preferred_element_type=F32)
 
+    ahead = spread.shape[0] == rows * lats
     acc = lax.fori_loop(
-        0, nlon // wide_step, gram_step, jnp.zeros((rows * lats, rows), F32)
+        0, nlon // wide_step, gram_step, jnp.zeros((rows * lats, rows), F32), unroll=ahead
     )
     gram[...] = acc * (1.0 / math.sqrt(2.0 * no * od) / math.sqrt(1.0 * nlon))
 
@@ -192,7 +195,6 @@
         both = jnp.concatenate([high, low], axis=1)
         return jnp.dot(both, fan[...], preferred_element_type=F32)
 
-    ahead = spread.shape[0] == rows * lats
     if ahead:
         spread[...] = expand(gram[...])
 
@@ -250,15 +252,23 @@
             out = t if out is None else jnp.where(part == s, t, out)
         pack(d, out.astype(BF16).astype(F32))
 
-    group = 2 * od * lats
+    group = od * lats
     if ahead:
+        def early(d, s, o):
+            at = ((s % 2) * no * od + d * od + s // 2) * lats
+            return spread[at : at + lats, o * LANES : (o + 1) * LANES]
         for d in range(no):
-            mix(d, lambda s, o: spread[d * group + s * lats : d * group + (s + 1) * lats, o * LANES : (o + 1) * LANES])
+            mix(d, functools.partial(early, d))
     else:
-        def late(d, c):
-            spread[...] = expand(gram[pl.ds(pl.multiple_of(d * group, group), group), :])
-            mix(d, lambda s, o: spread[s * lats : (s + 1) * lats, o * LANES : (o + 1) * LANES])
-            return c
+        def late(d, carry):
+            for c in range(2):
+                at = pl.multiple_of((c * no + d) * group, group)
+                spread[c * group : (c + 1) * group] = expand(gram[pl.ds(at, group), :])
+            def get(s, o):
+                at = (s % 2) * group + s // 2 * lats
+                return spread[at : at + lats, o * LANES : (o + 1) * LANES]
+            mix(d, get)
+            return carry
         lax.fori_loop(0, no, late, 0)
 
     vr[myf, me] = vs[myf, me]
@@ -303,6 +313,7 @@
                     stage[o, pl.ds(row, keep, stride=tiles2), :] = sums[
                         c * keep : (c + 1) * keep, t * LANES : (t + 1) * LANES
                     ]
+
         for b in range(keep):
             copy = pltpu.make_async_copy(
                 stage.at[o, pl.ds(b * tiles2, tiles2)], out.at[b, o], out_sem.at[o, b]
@@ -341,7 +352,6 @@
             pltpu.VMEM(harm.shape, BF16),
             pltpu.VMEM(leg.shape, BF16),
             pltpu.VMEM(noise_weight.shape, F32),
-            pltpu.VMEM((od, maps * tiles * 2, LANES), F32),
             pltpu.VMEM((rows, nlon), F32),
             pltpu.VMEM((rows, nlon), BF16),
             pltpu.VMEM((rows * lats, rows), F32),

time: 20.1 us -> 20.1 us (level)
  no operation moved by 1% of the time
where the time goes in v4:
time: 20.1 us; the launch traced here: 20 us
  Pallas kernels  18.1 us (90%)
  local copies, waits for them, and re-layouts  1.89 us (9%)
    pallas_call x1, Pallas kernels, on_device(): pl.pallas_call(functools.partial(gather_kernel, nf, no), out_shape=jax.Sh...  18.1 us
    unnamed x1, local copies, waits for them, and re-layouts  1.89 us

profile of v4, /device:TPU:0, one launch (start us, length us, event | category | flops | bytes accessed | tf_op | source)
XLA Modules:
  0.0 20.0 jit_solution(14923491109396287452)
XLA Ops:
  0.0 18.1 %operator.1 = f32[8,2,64,128]{3,2,1,0:T(8,128)} custom-call(s32[16]{0:T(128)} %ids_hbm.1, f32[4,4096]{1,0:T(4,128)} %beam_hbm.1, bf16[32,2,64,128]{3,2,1,0:T(8,128)(2,1)} %bitcast.12, bf16[2,64,4096]{2,1,0:T(8,128)(2,1)} %bitcast.13, f32[1,8,8192]{2,1,0:T(8,128)} %noise_hbm.1), custom_call_target="tpu_custom_call" | custom-call | tf_op jit(solution)/shard_map/operator/pallas_call | solution.py:344
  18.1 1.9 %copy.9 = f32[8,2,2,4096]{3,2,1,0:T(2,128)} copy(f32[8,2,2,4096]{3,2,1,0:T(2,128)} %bitcast.11) | data formatting | bytes 1048576

commit v5 on v4

--- a/solution.py
+++ b/solution.py
@@ -252,32 +252,37 @@
             out = t if out is None else jnp.where(part == s, t, out)
         pack(d, out.astype(BF16).astype(F32))
 
+    def copy2(f, o):
+        return pltpu.make_async_remote_copy(
+            vs.at[f, o], vr.at[myf, me], send2.at[f * no + o], recv2.at[lin],
+            device_id=(f, o), device_id_type=MESH,
+        )
+
     group = od * lats
-    if ahead:
-        def early(d, s, o):
-            at = ((s % 2) * no * od + d * od + s // 2) * lats
-            return spread[at : at + lats, o * LANES : (o + 1) * LANES]
-        for d in range(no):
-            mix(d, functools.partial(early, d))
-    else:
-        def late(d, carry):
+
+    def serve(d, own):
+        if ahead:
+            def get(s, o):
+                at = pl.multiple_of((s % 2) * no * group + d * group + s // 2 * lats, lats)
+                return spread[pl.ds(at, lats), o * LANES : (o + 1) * LANES]
+        else:
             for c in range(2):
                 at = pl.multiple_of((c * no + d) * group, group)
                 spread[c * group : (c + 1) * group] = expand(gram[pl.ds(at, group), :])
             def get(s, o):
                 at = (s % 2) * group + s // 2 * lats
                 return spread[at : at + lats, o * LANES : (o + 1) * LANES]
-            mix(d, get)
-            return carry
-        lax.fori_loop(0, no, late, 0)
-
+        mix(d, get)
+        for g in range(nf - 1 if own else nf):
+            copy2(wrap(myf + g + 1, nf), d).start()
+
+    if ahead:
+        for k in range(1, no):
+            serve(wrap(me + k, no), False)
+    else:
+        lax.fori_loop(1, no, lambda k, c: (serve(wrap(me + k, no), False), c)[1], 0)
+    serve(me, True)
     vr[myf, me] = vs[myf, me]
-
-    def copy2(f, o):
-        return pltpu.make_async_remote_copy(
-            vs.at[f, o], vr.at[myf, me], send2.at[f * no + o], recv2.at[lin],
-            device_id=(f, o), device_id_type=MESH,
-        )
 
     def arrive2(f, o):
         frm = f * no + o
@@ -286,7 +291,6 @@
             device_id=(f, o), device_id_type=MESH,
         ).wait_recv()
 
-    peers_all(lambda f, o: copy2(f, o).start())
     peers_all(arrive2)
 
     for f in range(nf):
@@ -323,6 +327,16 @@
 
     peers_order(lambda to: copy1(to).wait_send())
     peers_all(lambda f, o: copy2(f, o).wait_send())
+    for copy in copies:
+        copy.wait()
+
+
+def hand_over_kernel(source, out, sem):
+    copies = [
+        pltpu.make_async_copy(source.at[b], out.at[b], sem.at[b]) for b in range(source.shape[0])
+    ]
+    for copy in copies:
+        copy.start()
     for copy in copies:
         copy.wait()
 
@@ -376,6 +390,15 @@
         ),
         name="operator",
     )(order_ids, beam_window, harm, leg, noise_weight)
+    out = pl.pallas_call(
+        hand_over_kernel,
+        out_shape=jax.ShapeDtypeStruct(out.shape, out.dtype),
+        in_specs=[hbm],
+        out_specs=hbm,
+        scratch_shapes=[dma((keep,))],
+        compiler_params=pltpu.CompilerParams(vmem_limit_bytes=60 * 2**20),
+        name="hand_over",
+    )(out)
     out = jnp.swapaxes(out.reshape(keep, od, tiles, 2, LANES), 2, 3)
     return out.reshape(keep, od, 2, degrees)
 

time: 20.1 us -> 35.2 us (1.75)
  Pallas kernels: 18.1 us -> 35 us
  local copies, waits for them, and re-layouts: 1.89 us -> 0 us
    pallas_call x0 -> x1, Pallas kernels: none -> 17.1 us  [on_device(): pl.pallas_call(hand_over_kernel, out_shape=jax.ShapeDtypeStruct(out.shape...]
    unnamed x1 -> x0, local copies, waits for them, and re-layouts: 1.89 us -> none
where the time goes in v5:
time: 35.2 us; the launch traced here: 35 us
  Pallas kernels  35 us (99%)
    pallas_call x1, Pallas kernels, on_device(): pl.pallas_call(functools.partial(gather_kernel, nf, no), out_shape=jax.Sh...  18 us
    pallas_call x1, Pallas kernels, on_device(): pl.pallas_call(hand_over_kernel, out_shape=jax.ShapeDtypeStruct(out.shape...  17.1 us

profile of v5, /device:TPU:0, one launch (start us, length us, event | category | flops | bytes accessed | tf_op | source)
XLA Modules:
  0.0 35.0 jit_solution(1877702430324745845)
XLA Ops:
  0.0 18.0 %operator.1.source = f32[8,2,64,128]{3,2,1,0:T(8,128)} custom-call(s32[16]{0:T(128)} %ids_hbm.1, f32[4,4096]{1,0:T(4,128)} %beam_hbm.1, bf16[32,2,64,128]{3,2,1,0:T(8,128)(2,1)} %bitcast.11, bf16[2,64,4096]{2,1,0:T(8,128)(2,1)} %bitcast.12, f32[1,8,8192]{2,1,0:T(8,128)} %noise_hbm.1), custom_call_target="tpu_custom_call" | custom-call | tf_op jit(solution)/shard_map/operator/pallas_call | solution.py:358
  18.0 17.1 %hand_over.1 = f32[8,2,64,128]{3,2,1,0:T(8,128)} custom-call(f32[8,2,64,128]{3,2,1,0:T(8,128)} %operator.1.source), custom_call_target="tpu_custom_call" | custom-call | tf_op jit(solution)/shard_map/hand_over/pallas_call | solution.py:393

commit v6 on v4

--- a/solution.py
+++ b/solution.py
@@ -324,6 +324,19 @@
     peers_order(lambda to: copy1(to).wait_send())
     peers_all(lambda f, o: copy2(f, o).wait_send())
     for copy in copies:
+        copy.wait()
+
+
+def hand_over_kernel(source, out, held, sem_in, sem_out):
+    keep = source.shape[0]
+    fetch = [pltpu.make_async_copy(source.at[b], held.at[b], sem_in.at[b]) for b in range(keep)]
+    store = [pltpu.make_async_copy(held.at[b], out.at[b], sem_out.at[b]) for b in range(keep)]
+    for copy in fetch:
+        copy.start()
+    for b in range(keep):
+        fetch[b].wait()
+        store[b].start()
+    for copy in store:
         copy.wait()
 
 
@@ -376,6 +389,15 @@
         ),
         name="operator",
     )(order_ids, beam_window, harm, leg, noise_weight)
+    out = pl.pallas_call(
+        hand_over_kernel,
+        out_shape=jax.ShapeDtypeStruct(out.shape, out.dtype),
+        in_specs=[hbm],
+        out_specs=hbm,
+        scratch_shapes=[pltpu.VMEM(out.shape, F32), dma((keep,)), dma((keep,))],
+        compiler_params=pltpu.CompilerParams(vmem_limit_bytes=60 * 2**20),
+        name="hand_over",
+    )(out)
     out = jnp.swapaxes(out.reshape(keep, od, tiles, 2, LANES), 2, 3)
     return out.reshape(keep, od, 2, degrees)
 

time: 20.1 us -> 20.1 us (level)
  local copies, waits for them, and re-layouts: 1.89 us -> 0 us
  Pallas kernels: 18.1 us -> 19.9 us
    unnamed x1 -> x0, local copies, waits for them, and re-layouts: 1.89 us -> none
    pallas_call x0 -> x1, Pallas kernels: none -> 1.83 us  [on_device(): pl.pallas_call(hand_over_kernel, out_shape=jax.ShapeDtypeStruct(out.shape...]
where the time goes in v6:
time: 20.1 us; the launch traced here: 19.9 us
  Pallas kernels  19.9 us (99%)
    pallas_call x1, Pallas kernels, on_device(): pl.pallas_call(functools.partial(gather_kernel, nf, no), out_shape=jax.Sh...  18.1 us
    pallas_call x1, Pallas kernels, on_device(): pl.pallas_call(hand_over_kernel, out_shape=jax.ShapeDtypeStruct(out.shape...  1.83 us

profile of v6, /device:TPU:0, one launch (start us, length us, event | category | flops | bytes accessed | tf_op | source)
XLA Modules:
  0.0 19.9 jit_solution(10784031594955732719)
XLA Ops:
  0.0 18.1 %operator.1.source = f32[8,2,64,128]{3,2,1,0:T(8,128)} custom-call(s32[16]{0:T(128)} %ids_hbm.1, f32[4,4096]{1,0:T(4,128)} %beam_hbm.1, bf16[32,2,64,128]{3,2,1,0:T(8,128)(2,1)} %bitcast.11, bf16[2,64,4096]{2,1,0:T(8,128)(2,1)} %bitcast.12, f32[1,8,8192]{2,1,0:T(8,128)} %noise_hbm.1), custom_call_target="tpu_custom_call" | custom-call | tf_op jit(solution)/shard_map/operator/pallas_call | solution.py:357
  18.1 1.8 %hand_over.1 = f32[8,2,64,128]{3,2,1,0:T(8,128)} custom-call(f32[8,2,64,128]{3,2,1,0:T(8,128)} %operator.1.source), custom_call_target="tpu_custom_call" | custom-call | tf_op jit(solution)/shard_map/hand_over/pallas_call | solution.py:392

commit v7 on v6

--- a/solution.py
+++ b/solution.py
@@ -287,9 +287,11 @@
         ).wait_recv()
 
     peers_all(lambda f, o: copy2(f, o).start())
-    peers_all(arrive2)
-
-    for f in range(nf):
+
+    for g in range(nf):
+        f = wrap(myf + g, nf)
+        low = 1 if g == 0 else 0
+        lax.fori_loop(low, no, lambda k, c: (arrive2(f, wrap(me + k, no)), c)[1], 0, unroll=no <= 16)
         flipped[f] = jnp.concatenate([unpack(f, o) for o in range(no)], axis=0).T
 
     width = 1024

time: 20.1 us -> 20.7 us (1.030)
  Pallas kernels: 19.9 us -> 20.5 us
    pallas_call x1, Pallas kernels: 18.1 us -> 18.7 us  [on_device(): pl.pallas_call(functools.partial(gather_kernel, nf, no), out_shape=jax.Sh...]
where the time goes in v7:
time: 20.7 us; the launch traced here: 20.5 us
  Pallas kernels  20.5 us (99%)
    pallas_call x1, Pallas kernels, on_device(): pl.pallas_call(functools.partial(gather_kernel, nf, no), out_shape=jax.Sh...  18.7 us
    pallas_call x1, Pallas kernels, on_device(): pl.pallas_call(hand_over_kernel, out_shape=jax.ShapeDtypeStruct(out.shape...  1.83 us

profile of v7, /device:TPU:0, one launch (start us, length us, event | category | flops | bytes accessed | tf_op | source)
XLA Modules:
  0.0 20.5 jit_solution(6366178777554789277)
XLA Ops:
  0.0 18.7 %operator.1.source = f32[8,2,64,128]{3,2,1,0:T(8,128)} custom-call(s32[16]{0:T(128)} %ids_hbm.1, f32[4,4096]{1,0:T(4,128)} %beam_hbm.1, bf16[32,2,64,128]{3,2,1,0:T(8,128)(2,1)} %bitcast.11, bf16[2,64,4096]{2,1,0:T(8,128)(2,1)} %bitcast.12, f32[1,8,8192]{2,1,0:T(8,128)} %noise_hbm.1), custom_call_target="tpu_custom_call" | custom-call | tf_op jit(solution)/shard_map/operator/pallas_call | solution.py:359
  18.7 1.8 %hand_over.1 = f32[8,2,64,128]{3,2,1,0:T(8,128)} custom-call(f32[8,2,64,128]{3,2,1,0:T(8,128)} %operator.1.source), custom_call_target="tpu_custom_call" | custom-call | tf_op jit(solution)/shard_map/hand_over/pallas_call | solution.py:394
